TPU v7x, 32 devices: a whole 2x2x4 slice. The times are simulated.
32 devices in a mesh: dp: 8 (over y, x, core), tensor: 4 (over z).
Axes of the slice: x: 2, y: 2, z: 4, core: 2. Of those that a mesh axis runs over, the one named last changes fastest.
Arguments:
- tokens: bfloat16 [4096, 768], P('dp'), may hold values from -6 to 6
- segments: int32 [16, 256], P('dp'), may hold values from 0 to 3, never falling along the last dimension, each value on 1 to 128 neighbouring positions
- cotangent: bfloat16 [4096, 768], P('dp'), may hold values from -6 to 6
- w_qkv: float32 [3, 768, 768], P(None, None, 'tensor'), may hold values from -0.21875 to 0.21875
- w_out: float32 [768, 768], P('tensor'), may hold values from -0.625 to 0.625
- w_up: float32 [768, 3072], P(None, 'tensor'), may hold values from -0.21875 to 0.21875
- w_down: float32 [3072, 768], P('tensor'), may hold values from -0.109375 to 0.109375
- head_bias: float32 [2, 768], P(None, 'tensor'), may hold values from -1.8 to 1.8
- ff_bias: float32 [3072], P('tensor'), may hold values from -1.8 to 1.8
- row_params: float32 [6, 768], replicated
- mom_qkv: float32 [3, 768, 768], P(None, None, 'tensor')
- mom_out: float32 [768, 768], P('tensor')
- mom_up: float32 [768, 3072], P(None, 'tensor')
- mom_down: float32 [3072, 768], P('tensor')
- mom_heads: float32 [2, 768], P(None, 'tensor')
- mom_ff: float32 [3072], P('tensor')
- mom_params: float32 [6, 768], replicated, may hold values from -192 to 192
Outputs:
- layer_out: bfloat16 [4096, 768], P('dp')
- grad_tokens: bfloat16 [4096, 768], P('dp')
- new_mom_qkv: float32 [3, 768, 768], P(None, None, 'tensor')
- new_qkv: float32 [3, 768, 768], P(None, None, 'tensor')
- low_qkv: bfloat16 [3, 768, 768], P(None, None, 'tensor')
- new_mom_out: float32 [768, 768], P('tensor')
- new_out: float32 [768, 768], P('tensor')
- low_out: bfloat16 [768, 768], P('tensor')
- new_mom_up: float32 [768, 3072], P(None, 'tensor')
- new_up: float32 [768, 3072], P(None, 'tensor')
- low_up: bfloat16 [768, 3072], P(None, 'tensor')
- new_mom_down: float32 [3072, 768], P('tensor')
- new_down: float32 [3072, 768], P('tensor')
- low_down: bfloat16 [3072, 768], P('tensor')
- new_mom_heads: float32 [2, 768], P(None, 'tensor')
- new_heads: float32 [2, 768], P(None, 'tensor')
- new_mom_ff: float32 [3072], P('tensor')
- new_ff: float32 [3072], P('tensor')
- new_mom_params: float32 [6, 768], replicated
- new_params: float32 [6, 768], replicated
Inputs may be any that keep to these rules, and one draw needn't show every extreme that they name: `segments`: within each row of 256 positions the numbers never fall; each number present covers 1 to 128 positions, and one covers exactly 128.
All inputs are finite; a program needn't handle non-finite values.
Results may differ from a plain program's by a relative error of at most 0.024.
Values may be sent and summed in bfloat16 or wider, within the bound.
A program may use at most 192 MiB of HBM per device.

v0:
```python
import functools
import math

import jax
import jax.numpy as jnp
from jax import lax
from jax.experimental import pallas as pl
from jax.experimental.pallas import tpu as pltpu
from jax.sharding import PartitionSpec as P

HD = 64
EPS_NORM = 1e-05
coef_a = 3.4445
coef_b = -4.775
coef_c = 2.0315
BF = jnp.bfloat16
F32 = jnp.float32
MESH = pl.DeviceIdType.MESH
SUBS = 2
PLACE = (1, 2, 0, 3)
CUTS = 3


def remote(src, dst, send_sem, recv_sem, device):
    return pltpu.make_async_remote_copy(
        src_ref=src,
        dst_ref=dst,
        send_sem=send_sem,
        recv_sem=recv_sem,
        device_id=device,
        device_id_type=MESH,
    )


def greet(devices):
    barrier = pltpu.get_barrier_semaphore()
    for device in devices:
        pl.semaphore_signal(barrier, inc=1, device_id=device, device_id_type=MESH)
    pl.semaphore_wait(barrier, len(devices))


def z_peers(t):
    return [{"tensor": (t + k) % 4} for k in range(1, 4)]


def line_scratch(rows, width, dtype):
    part = rows // 4
    return [
        pltpu.VMEM((part, width), dtype),
        pltpu.VMEM((part, width), dtype),
        pltpu.VMEM((2 * part, width), dtype),
        pltpu.VMEM((2 * part, width), dtype),
        pltpu.SemaphoreType.DMA((8 * SUBS,)),
        pltpu.SemaphoreType.DMA((8 * SUBS,)),
    ]


def line_sum(t, x, o, scratch):
    raw, cmb, fwd, mix, ssem, rsem = scratch
    part = raw.shape[0]
    half = part // SUBS
    subs = range(SUBS)
    mate = t + 1 - 2 * (t % 2)
    outer = (t % 3) == 0
    inner = (t % 3) != 0

    def at(ref, chunk, s):
        return ref.at[pl.ds(pl.multiple_of(chunk * part + s * half, half), half)]

    def to(index, src, dst, recv, device):
        return remote(src, dst, ssem.at[index], rsem.at[recv], {"tensor": device})

    def ag_sem(chunk, s):
        return (4 + chunk) * SUBS + s

    def o_far(s):
        return to(s, at(x, 3 - t, s), at(fwd, 0, s), 2 * SUBS + s, mate)

    def o_near(s):
        return to(SUBS + s, at(x, 3 - mate, s), at(fwd, 1, s), 3 * SUBS + s, mate)

    def o_raw(s):
        return to(2 * SUBS + s, at(x, mate, s), at(raw, 0, s), s, mate)

    def o_own(s):
        return to(3 * SUBS + s, at(o, t, s), at(o, t, s), ag_sem(t, s), mate)

    def i_raw(s):
        return to(s, at(x, mate, s), at(raw, 0, s), s, mate)

    def i_far(s):
        return to(SUBS + s, at(mix, 0, s), at(cmb, 0, s), SUBS + s, 3 - mate)

    def i_near(s):
        return to(2 * SUBS + s, at(mix, 1, s), at(cmb, 0, s), SUBS + s, 3 - t)

    def i_ag(place, chunk, s, device):
        return to(place * SUBS + s, at(o, chunk, s), at(o, chunk, s), ag_sem(chunk, s), device)

    def got(dst, recv):
        remote(dst, dst, ssem.at[0], rsem.at[recv], {"tensor": mate}).wait_recv()

    def add(dst, *terms):
        total = terms[0][...].astype(F32)
        for term in terms[1:]:
            total = total + term[...].astype(F32)
        dst[...] = total.astype(dst.dtype)

    def start():
        @pl.when(outer)
        def _():
            for build in (o_far, o_near, o_raw):
                for s in subs:
                    build(s).start()

        @pl.when(inner)
        def _():
            for s in subs:
                i_raw(s).start()

    def combine():
        @pl.when(inner)
        def _():
            for slot, chunk, build in ((0, 3 - mate, i_far), (1, 3 - t, i_near)):
                for s in subs:
                    got(at(fwd, slot, s), (2 + slot) * SUBS + s)
                    add(at(mix, slot, s), at(fwd, slot, s), at(x, chunk, s))
                    build(s).start()

    def settle():
        for s in subs:
            got(at(raw, 0, s), s)
            got(at(cmb, 0, s), SUBS + s)
            add(at(o, t, s), at(x, t, s), at(raw, 0, s), at(cmb, 0, s))

            @pl.when(outer)
            def _(s=s):
                o_own(s).start()

            @pl.when(inner)
            def _(s=s):
                i_ag(3, t, s, 3 - t).start()
                i_ag(4, t, s, mate).start()

    def pass_on():
        @pl.when(inner)
        def _():
            for s in subs:
                got(at(o, mate, s), ag_sem(mate, s))
                i_ag(5, mate, s, 3 - t).start()
            for s in subs:
                got(at(o, 3 - t, s), ag_sem(3 - t, s))
                i_ag(6, 3 - t, s, mate).start()
            for s in subs:
                got(at(o, 3 - mate, s), ag_sem(3 - mate, s))
                i_ag(7, 3 - mate, s, mate).start()

    def finish():
        @pl.when(outer)
        def _():
            for chunk in (mate, 3 - mate, 3 - t):
                for s in subs:
                    got(at(o, chunk, s), ag_sem(chunk, s))
            for build in (o_far, o_near, o_raw, o_own):
                for s in subs:
                    build(s).wait_send()

        @pl.when(inner)
        def _():
            for s in subs:
                for build in (i_raw, i_far, i_near):
                    build(s).wait_send()
                i_ag(3, t, s, 3 - t).wait_send()
                i_ag(4, t, s, mate).wait_send()
                i_ag(5, mate, s, 3 - t).wait_send()
                i_ag(6, 3 - t, s, mate).wait_send()
                i_ag(7, 3 - mate, s, mate).wait_send()

    return [start, combine, settle, pass_on, finish]


def relay_scratch(rows, width, dtype):
    part = rows // 2
    return [
        pltpu.VMEM((2 * part, width), dtype),
        pltpu.VMEM((part, width), dtype),
        pltpu.VMEM((part, width), dtype),
        pltpu.SemaphoreType.DMA((5 * SUBS,)),
        pltpu.SemaphoreType.DMA((5 * SUBS,)),
    ]


def relay_sum(t, x, o, scratch):
    taken, mixed, mix, ssem, rsem = scratch
    part = mixed.shape[0]
    piece = part // SUBS
    subs = range(SUBS)
    mate = t + 1 - 2 * (t % 2)
    facing = 3 - t
    outer = (t % 3) == 0
    inner = (t % 3) != 0
    near = t // 2
    far = 1 - near

    def at(ref, chunk, s):
        return ref.at[pl.ds(pl.multiple_of(chunk * part + s * piece, piece), piece)]

    def to(index, src, dst, recv, device):
        return remote(
            src, dst, ssem.at[index], rsem.at[recv], {"tensor": device}
        )

    def give_far(s):
        return to(s, at(x, far, s), at(taken, 0, s), s, mate)

    def give_near(s):
        return to(SUBS + s, at(x, near, s), at(taken, 1, s), SUBS + s, mate)

    def cross(s):
        return to(s, at(mix, 0, s), at(mixed, 0, s), 2 * SUBS + s, facing)

    def own_across(s):
        return to(SUBS + s, at(o, near, s), at(o, near, s), (3 + near) * SUBS + s, facing)

    def own_out(s):
        return to(2 * SUBS + s, at(o, near, s), at(o, near, s), (3 + near) * SUBS + s, mate)

    def far_out(s):
        return to(3 * SUBS + s, at(o, far, s), at(o, far, s), (3 + far) * SUBS + s, mate)

    def got(dst, recv):
        remote(dst, dst, ssem.at[0], rsem.at[recv], {"tensor": mate}).wait_recv()

    def add(dst, *terms):
        total = terms[0][...].astype(F32)
        for term in terms[1:]:
            total = total + term[...].astype(F32)
        dst[...] = total.astype(dst.dtype)

    def start():
        @pl.when(outer)
        def _():
            for build in (give_far, give_near):
                for s in subs:
                    build(s).start()

    def combine():
        @pl.when(inner)
        def _():
            for s in subs:
                got(at(taken, 0, s), s)
                add(at(mix, 0, s), at(taken, 0, s), at(x, far, s))
                cross(s).start()

    def settle():
        @pl.when(inner)
        def _():
            for s in subs:
                got(at(taken, 1, s), SUBS + s)
                got(at(mixed, 0, s), 2 * SUBS + s)
                add(at(o, near, s), at(x, near, s), at(taken, 1, s), at(mixed, 0, s))
                own_across(s).start()
                own_out(s).start()

    def pass_on():
        @pl.when(inner)
        def _():
            for s in subs:
                got(at(o, far, s), (3 + far) * SUBS + s)
                far_out(s).start()

    def finish():
        @pl.when(outer)
        def _():
            for chunk in (near, far):
                for s in subs:
                    got(at(o, chunk, s), (3 + chunk) * SUBS + s)
            for build in (give_far, give_near):
                for s in subs:
                    build(s).wait_send()

        @pl.when(inner)
        def _():
            for build in (cross, own_across, own_out, far_out):
                for s in subs:
                    build(s).wait_send()

    return [start, combine, settle, pass_on, finish]


def params(collective_id, mebibytes):
    return pltpu.CompilerParams(
        collective_id=collective_id,
        has_side_effects=True,
        vmem_limit_bytes=mebibytes * 1024 * 1024,
    )


IN_VMEM = pl.BlockSpec(memory_space=pltpu.VMEM)
IN_HBM = pl.BlockSpec(memory_space=pltpu.HBM)


def plane_scratch(count, rows, width):
    pairs = count // 2
    side = width // 2
    block = rows // pairs
    return [
        pltpu.VMEM((rows, side), BF),
        pltpu.VMEM((rows, side), BF),
        pltpu.VMEM((pairs, block, side), BF),
        pltpu.SemaphoreType.DMA((5, pairs)),
        pltpu.SemaphoreType.DMA((4, pairs)),
    ]


def plane_sum(count, p, x, o, scratch):
    from_mate, paired, slots, ssem, rsem = scratch
    pairs = count // 2
    side = from_mate.shape[1]
    block = slots.shape[1]
    pair = p // 2
    core = p % 2
    mate = {"dp": p + 1 - 2 * core}

    def rows_of(index):
        return pl.ds(pl.multiple_of(index * block, block), block)

    def cols_of(which):
        return pl.ds(pl.multiple_of(which * side, side), side)

    def after(k):
        return (pair + k) % pairs

    def before(k):
        return (pair + pairs - k) % pairs

    def give(k):
        spot = rows_of(after(k))
        return remote(
            x.at[spot, cols_of(1 - core)], from_mate.at[spot], ssem.at[0, k % pairs], rsem.at[0, k % pairs], mate
        )

    def hand(k):
        spot = rows_of(after(k))
        return remote(
            paired.at[spot], slots.at[k], ssem.at[1, k], rsem.at[1, k], {"dp": 2 * after(k) + core}
        )

    def spread(k):
        spot = o.at[rows_of(pair), cols_of(core)]
        return remote(spot, spot, ssem.at[2, k], rsem.at[2, k], {"dp": 2 * after(k) + core})

    def share(k):
        spot = o.at[rows_of(before(k)), cols_of(core)]
        return remote(spot, spot, ssem.at[3, k], rsem.at[3, k], mate)

    def start():
        for k in range(1, pairs + 1):
            give(k).start()

    def pair_up():
        for k in range(1, pairs + 1):
            spot = rows_of(after(k))
            give(k).wait_recv()
            total = x[spot, cols_of(core)].astype(F32) + from_mate[spot].astype(F32)
            paired[spot] = total.astype(BF)
            if k < pairs:
                hand(k).start()

    def settle():
        spot = rows_of(pair)
        total = paired[spot].astype(F32)
        for k in range(1, pairs):
            hand(k).wait_recv()
            total = total + slots[k].astype(F32)
        o[spot, cols_of(core)] = total.astype(BF)
        for k in range(1, pairs):
            spread(k).start()
        share(0).start()

    def pass_on():
        for k in range(1, pairs):
            spot = o.at[rows_of(before(k)), cols_of(core)]
            remote(spot, spot, ssem.at[2, k], rsem.at[2, k], mate).wait_recv()
            share(k).start()

    def finish():
        for k in range(pairs):
            spot = o.at[rows_of(before(k)), cols_of(1 - core)]
            remote(spot, spot, ssem.at[3, k], rsem.at[3, k], mate).wait_recv()
        for k in range(1, pairs + 1):
            give(k).wait_send()
        for k in range(1, pairs):
            hand(k).wait_send()
            spread(k).wait_send()
        for k in range(pairs):
            share(k).wait_send()

    return [start, pair_up, settle, pass_on, finish]


def reduce_scratch(rows, width):
    side = width // 2
    return [
        pltpu.VMEM((rows, side), BF),
        pltpu.VMEM((rows, side), BF),
        pltpu.VMEM((2 * rows, side), BF),
        pltpu.SemaphoreType.DMA((2, 8)),
        pltpu.SemaphoreType.DMA((2, 8)),
    ]


def square_reduce(p, x, kept, matrices, scratch):
    from_mate, paired, taken, ssem, rsem = scratch
    side = from_mate.shape[1]
    pair = p // 2
    core = p % 2
    mate = {"dp": p + 1 - 2 * core}

    def away_from(place, away):
        return {"dp": 2 * (place ^ away) + core}

    def cols_of(which):
        return pl.ds(pl.multiple_of(which * side, side), side)

    def give(m):
        _, first, rows = matrices[m]
        spot = pl.ds(first, rows)
        return remote(x.at[spot, cols_of(1 - core)], from_mate.at[spot], ssem.at[m, 0], rsem.at[m, 0], mate)

    def part_of(m, part):
        _, first, rows = matrices[m]
        return pl.ds(first + part * (rows // 2), rows // 2)

    def slot(m, near, part):
        _, first, rows = matrices[m]
        return pl.ds(2 * first + near * rows + part * (rows // 2), rows // 2)

    def opposite_send(m, part):
        place = matrices[m][0]
        return remote(
            paired.at[part_of(m, part)], taken.at[slot(m, 0, part)],
            ssem.at[m, 1 + part], rsem.at[m, 1], away_from(place, 1 + part),
        )

    def near_raw(m, near):
        part = 1 - near
        return remote(
            paired.at[part_of(m, part)], taken.at[slot(m, near, part)],
            ssem.at[m, 1], rsem.at[m, 2 + 2 * near], away_from(matrices[m][0], 0),
        )

    def near_mixed(m, near):
        part = near
        return remote(
            paired.at[part_of(m, part)], taken.at[slot(m, near, part)],
            ssem.at[m, 2], rsem.at[m, 3 + 2 * near], away_from(matrices[m][0], 0),
        )

    def swap(m):
        spot = kept.at[pl.ds(0, matrices[m][2]), cols_of(core)]
        return remote(spot, spot, ssem.at[m, 6], rsem.at[m, 6], mate)

    def arrived(ref, m, index):
        remote(ref, ref, ssem.at[m, 0], rsem.at[m, index], mate).wait_recv()

    def role(m, away):
        return pl.when(pair == (matrices[m][0] ^ away))

    every = range(len(matrices))

    def start():
        for m in every:
            give(m).start()

    def pair_up():
        for m in every:
            _, first, rows = matrices[m]
            spot = pl.ds(first, rows)
            give(m).wait_recv()
            total = x[spot, cols_of(core)].astype(F32) + from_mate[spot].astype(F32)
            paired[spot] = total.astype(BF)

            @role(m, 3)
            def _(m=m):
                for part in range(2):
                    opposite_send(m, part).start()

            for near in range(2):

                @role(m, 1 + near)
                def _(m=m, near=near):
                    near_raw(m, near).start()

    def mix():
        for m in every:
            for near in range(2):

                @role(m, 1 + near)
                def _(m=m, near=near):
                    piece = slot(m, 0, near)
                    arrived(taken.at[piece], m, 1)
                    spot = part_of(m, near)
                    total = paired[spot].astype(F32) + taken[piece].astype(F32)
                    paired[spot] = total.astype(BF)
                    near_mixed(m, near).start()

    def settle():
        for m in every:

            @role(m, 0)
            def _(m=m):
                _, first, rows = matrices[m]
                for near in range(2):
                    arrived(taken.at[slot(m, near, 1 - near)], m, 2 + 2 * near)
                    arrived(taken.at[slot(m, near, near)], m, 3 + 2 * near)
                spot = pl.ds(first, rows)
                total = x[spot, cols_of(core)].astype(F32) + from_mate[spot].astype(F32)
                for near in range(2):
                    total = total + taken[pl.ds(2 * first + near * rows, rows)].astype(F32)
                kept[pl.ds(0, rows), cols_of(core)] = total.astype(BF)
                swap(m).start()

    def finish():
        for m in every:
            rows = matrices[m][2]
            give(m).wait_send()

            @role(m, 0)
            def _(m=m, rows=rows):
                arrived(kept.at[pl.ds(0, rows), cols_of(1 - core)], m, 6)
                swap(m).wait_send()

            @role(m, 3)
            def _(m=m):
                for part in range(2):
                    opposite_send(m, part).wait_send()

            for near in range(2):

                @role(m, 1 + near)
                def _(m=m, near=near):
                    near_raw(m, near).wait_send()
                    near_mixed(m, near).wait_send()

    return [start, pair_up, mix, settle, finish]


def gather_scratch():
    return [pltpu.SemaphoreType.DMA((4, 2 * CUTS, 4))] * 2


def square_gather(p, sizes, out, own, cuts, scratch):
    ssem, rsem = scratch
    width = out.shape[1]
    pair = p // 2
    core = p % 2
    mate = {"dp": p + 1 - 2 * core}
    firsts = [sum(sizes[:index]) for index in range(4)]

    def piece(index, side, part):
        rows = sizes[index]
        if index == 2:
            across = pl.ds(pl.multiple_of(side * (width // 2), width // 2), width // 2)
            share = rows // (2 * cuts)
            return out.at[pl.ds(firsts[index] + part * share, share), across]
        share = rows // (4 * cuts)
        first = firsts[index] + side * (rows // 2) + part * share
        return out.at[pl.ds(pl.multiple_of(first, share), share)]

    def copy(index, part, route, device):
        spot = piece(index, core, part)
        return remote(spot, spot, ssem.at[index, part, route], rsem.at[index, part, route], device)

    def other(away):
        return {"dp": 2 * (pair + away * (1 - 2 * ((pair // away) % 2))) + core}

    def role(index, away):
        return pl.when(pair == (PLACE[index] ^ away))

    def wait_in(index, part, route, side):
        spot = piece(index, side, part)
        remote(spot, spot, ssem.at[index, part, route], rsem.at[index, part, route], mate).wait_recv()

    ways = ((1, 0, 2), (2, 1, 1))
    parts = 2 * cuts

    def half(which):
        return range(which * cuts, (which + 1) * cuts)

    def start():
        for index in range(4):

            @role(index, 0)
            def _(index=index):
                for part in range(parts):
                    piece(index, core, part)[...] = own(index, part)
                for part in range(parts):
                    copy(index, part, 0, other(1)).start()
                    copy(index, (part + cuts) % parts, 1, other(2)).start()
                for part in range(parts):
                    copy(index, part, 3, mate).start()

    def pass_on(indices=range(4)):
        for index in indices:
            for away, route, onward in ways:

                @role(index, away)
                def _(index=index, away=away, route=route, onward=onward):
                    for part in half(away - 1):
                        wait_in(index, part, route, core)
                        copy(index, part, 2, other(onward)).start()
                        copy(index, part, 3, mate).start()

    def rest():
        for index in range(4):
            for away, route, _ in ways:

                @role(index, away)
                def _(index=index, away=away, route=route):
                    for part in half(2 - away):
                        wait_in(index, part, route, core)
                        copy(index, part, 3, mate).start()

            @role(index, 3)
            def _(index=index):
                for part in [part // 2 + cuts * (part % 2) for part in range(parts)]:
                    wait_in(index, part, 2, core)
                    copy(index, part, 3, mate).start()

    def finish():
        for index in range(4):
            for part in range(parts):
                wait_in(index, part, 3, 1 - core)
                copy(index, part, 3, mate).wait_send()

            @role(index, 0)
            def _(index=index):
                for part in range(parts):
                    copy(index, part, 0, other(1)).wait_send()
                    copy(index, part, 1, other(2)).wait_send()

            for away, _, onward in ways:

                @role(index, away)
                def _(index=index, away=away, onward=onward):
                    for part in half(away - 1):
                        copy(index, part, 2, other(onward)).wait_send()

    return [start, pass_on, rest, finish]


def vector_scratch(count, shape):
    return [
        pltpu.VMEM((count,) + shape, F32),
        pltpu.SemaphoreType.DMA((count,)),
        pltpu.SemaphoreType.DMA((count,)),
    ]


def vector_sum(axis, count, p, v, o, scratch):
    slots, ssem, rsem = scratch

    def send(k):
        return remote(v, slots.at[p], ssem.at[k], rsem.at[k], {axis: (p + k) % count})

    def start():
        slots[p] = v[...]
        for k in range(1, count):
            send(k).start()

    def finish():
        for k in range(1, count):
            spot = slots.at[(p + count - k) % count]
            remote(v, spot, ssem.at[k], rsem.at[k], {axis: (p + k) % count}).wait_recv()
        total = slots[0]
        for k in range(1, count):
            total = total + slots[k]
        o[...] = total
        for k in range(1, count):
            send(k).wait_send()

    return [start, finish]


ROW_STEP = 32


def tdot(left, right):
    return lax.dot_general(left, right, (((0,), (0,)), ((), ())), preferred_element_type=F32)


def dot(left, right):
    return jnp.dot(left, right, preferred_element_type=F32)


def dot_t(left, right):
    return lax.dot_general(left, right, (((1,), (1,)), ((), ())), preferred_element_type=F32)


def cut(values):
    high = values.astype(BF)
    return high, (values - high.astype(F32)).astype(BF)


def dot3(lh, ll, rh, rl, dims=(((1,), (0,)), ((), ()))):
    def dot(left, right):
        return lax.dot_general(left, right, dims, preferred_element_type=F32)

    return dot(lh, rh) + (dot(lh, rl) + dot(ll, rh))


def step_kernel(
    count, sizes,
    seg, rp, hb, fb, mh, mf, x_hbm, cot_hbm, wq_hbm, wo_hbm, wu_hbm, wd_hbm, mq, mo, mu, md,
    y_hbm, gt_hbm, xo_hbm, gall_hbm, vec, totals,
    y, gt, xo, gall, x, cot, f1, f2, f3, f4, wo_f, gx, go, gp, dz1, b1, b2, b3, b4, b5, b6, b7, b8, bt, red_s, kept,
    gap, gbp, wq, wo, q_s, k_s, v_s, ctx_s, dq_s, dk_s, dv_s, p_s, inv1_s, vecp, squares,
    wsem, lsem, psem, osem, *scratch,
):
    p = lax.axis_index("dp")
    t = lax.axis_index("tensor")
    tokens, width = x.shape
    half = tokens // 2
    quarter = tokens // 4
    columns = q_s.shape[1]
    heads = columns // HD
    tile = width // 3
    scale = 1.0 / math.sqrt(HD)
    square = count == 8
    group = count // 4
    share = width // group
    which = p // group
    core = p % 2
    mate = {"dp": p + 1 - 2 * core}
    firsts = [sum(sizes[:index]) for index in range(4)]
    n1_s, slope_s, dz2_s, u_s = (ref.at[pl.ds(0, tokens)] for ref in (f3, f1, f2, f4))
    h1l_s, act_s, du_s, dm_s, da_s, part_s = (
        ref.at[pl.ds(0, tokens)] for ref in (b3, b4, b5, b6, b7, b8)
    )
    wu, wd = b1, b2
    zf, af, sf, xf = f3, f1, f2, f4.at[pl.ds(0, share)]
    ah, al, zh, zl, dh, dl, sh, sl = b1, b2, b3, b4, b5, b6, b7, b8
    gf = kept if square else gall
    loads = [
        pltpu.make_async_copy(source, target, wsem.at[i])
        for i, (source, target) in enumerate(
            (
                (wq_hbm, f4), (wo_hbm, wo_f), (wu_hbm, f1), (wd_hbm, f2),
                (x_hbm, x), (cot_hbm, cot),
            )
        )
    ]
    for place in (0, 4, 1, 2, 3, 5):
        loads[place].start()
    greet(z_peers(t) + [{"dp": (p + k) % count} for k in range(1, count)])
    sums, back = [], []
    for q in range(4):
        place = pl.ds(q * quarter, quarter)
        pieces = scratch[5 * q : 5 * q + 5]
        sums.append(relay_sum(t, part_s.at[place], red_s.at[place], pieces))
        back.append(relay_sum(t, bt.at[place], red_s.at[place], pieces))
    top = 4 * columns
    if square:
        ends = [(PLACE[2], 0, width), (PLACE[3], width, width)]
        plane_b = square_reduce(p, gbp, kept, ends, scratch[20:25])
        ends = [(PLACE[0], 0, 3 * columns), (PLACE[1], 3 * columns, columns)]
        plane_a = square_reduce(p, gap, kept, ends, scratch[25:30])
    else:
        plane_b = plane_sum(count, p, gbp, gall.at[pl.ds(top, 2 * width)], scratch[20:25])
        plane_a = plane_sum(count, p, gap, gall.at[pl.ds(0, top)], scratch[25:30])
    vector = vector_sum("dp", count, p, vecp, vec, scratch[30:33])
    along = vector_sum("tensor", 4, t, squares, totals, scratch[33:36])
    line = line_sum(t, gx, go, scratch[36:42])
    vecp[...] = jnp.zeros_like(vecp)
    lane = lax.broadcasted_iota(jnp.int32, (1, columns), 1)

    def in_head(index):
        return (lane // HD) == index

    def rows_of(h):
        return pl.ds(h * half, half)

    def quarter_of(q):
        return pl.ds(q * quarter, quarter)

    def over_rows(q, body, init=0):
        def step(i, carry):
            first = q * quarter + i * ROW_STEP
            return body(pl.ds(pl.multiple_of(first, ROW_STEP), ROW_STEP), carry)

        return lax.fori_loop(0, quarter // ROW_STEP, step, init)

    def fold(values):
        return values.reshape(ROW_STEP // 8, 8, values.shape[1]).sum(axis=0)

    def add_vec(row, folded):
        vecp[row : row + 1, 0 : folded.shape[1]] += jnp.sum(folded, axis=0, keepdims=True)

    def narrow(index, source, target):
        loads[index].wait()
        target[...] = source[...].astype(BF)

    def attention(h):
        r = rows_of(h)
        xb = x[r]
        q = (dot_t(xb, wq[0 * columns : 1 * columns]) + hb[0:1]).astype(BF)
        k = dot_t(xb, wq[1 * columns : 2 * columns]).astype(BF)
        v = (dot_t(xb, wq[2 * columns : 3 * columns]) + hb[1:2]).astype(BF)
        q_s[r], k_s[r], v_s[r] = q, k, v
        down = jnp.broadcast_to(seg[h : h + 1].astype(F32), (half, half))
        same = down == down.T

        def one_head(index, context):
            mine = jnp.where(in_head(index), q, jnp.zeros_like(q))
            scores = jnp.where(same, dot_t(mine, k) * scale, -1e30)
            expo = jnp.exp(scores - jnp.max(scores, axis=-1, keepdims=True))
            probs = expo / jnp.sum(expo, axis=-1, keepdims=True)
            p_s[h * heads + index] = probs
            return jnp.where(in_head(index), dot(probs.astype(BF), v), context)

        context = lax.fori_loop(0, heads, one_head, jnp.zeros((half, columns), F32))
        low = context.astype(BF)
        ctx_s[r] = low
        part_s[r] = dot(low, wo[...]).astype(BF)

    def up(q):
        def norm(r, carry):
            z = x[r].astype(F32) + red_s[r].astype(F32) + rp[0:1]
            center = z - jnp.mean(z, axis=-1, keepdims=True)
            inverse = lax.rsqrt(jnp.mean(center * center, axis=-1, keepdims=True) + EPS_NORM)
            normed = center * inverse
            n1_s[r] = normed
            inv1_s[r] = jnp.broadcast_to(inverse, (ROW_STEP, 128))
            h1l_s[r] = (normed * rp[2:3] + rp[3:4]).astype(BF)
            return carry

        over_rows(q, norm)
        u_s[quarter_of(q)] = dot(h1l_s[quarter_of(q)], wu[...])

        def gelu(r, carry):
            u = u_s[r] + fb[...].reshape(1, width)
            cdf = 0.5 * (1.0 + lax.erf(u * (1.0 / math.sqrt(2.0))))
            act_s[r] = (u * cdf).astype(BF)
            slope_s[r] = cdf + u * jnp.exp(-0.5 * u * u) * (1.0 / math.sqrt(2.0 * math.pi))
            return carry

        over_rows(q, gelu)

    def down(q):
        r = quarter_of(q)
        part_s[r] = dot(act_s[r], wd[...]).astype(BF)

    def out_back(q):
        def norm(r, carry):
            s_dz2, s_dyn, s_dy = carry
            h1 = n1_s[r] * rp[2:3] + rp[3:4]
            z = h1 + red_s[r].astype(F32) + rp[1:2]
            center = z - jnp.mean(z, axis=-1, keepdims=True)
            inverse = lax.rsqrt(jnp.mean(center * center, axis=-1, keepdims=True) + EPS_NORM)
            normed = center * inverse
            y[r] = (normed * rp[4:5] + rp[5:6]).astype(BF)
            dy = cot[r].astype(F32)
            scaled = dy * rp[4:5]
            first = jnp.mean(scaled, axis=-1, keepdims=True)
            second = jnp.mean(scaled * normed, axis=-1, keepdims=True)
            dz2 = inverse * (scaled - first - normed * second)
            dz2_s[r] = dz2
            dm_s[r] = dz2.astype(BF)
            return s_dz2 + fold(dz2), s_dyn + fold(dy * normed), s_dy + fold(dy)

        zero = jnp.zeros((8, width), F32)
        for row, total in zip((1, 4, 5), over_rows(q, norm, (zero, zero, zero))):
            add_vec(row, total)
        u_s[quarter_of(q)] = dot_t(dm_s[quarter_of(q)], wd[...])

        def slope(r, carry):
            du = (u_s[r] * slope_s[r]).astype(BF)
            du_s[r] = du
            return carry + fold(du.astype(F32))

        add_vec(6, over_rows(q, slope, zero))

    def up_back(q):
        r = quarter_of(q)
        part_s[r] = dot_t(du_s[r], wu[...]).astype(BF)

    def grads_b():
        gbp[0:width] = tdot(h1l_s[...], du_s[...]).astype(BF)
        gbp[width : 2 * width] = tdot(act_s[...], dm_s[...]).astype(BF)

    def norm_back(q):
        def norm(r, carry):
            s_dz1, s_dhn, s_dh = carry
            dh1 = red_s[r].astype(F32) + dz2_s[r]
            normed = n1_s[r]
            scaled = dh1 * rp[2:3]
            first = jnp.mean(scaled, axis=-1, keepdims=True)
            second = jnp.mean(scaled * normed, axis=-1, keepdims=True)
            grad = inv1_s[r][:, 0:1] * (scaled - first - normed * second)
            dz1[r] = grad
            da_s[r] = grad.astype(BF)
            return s_dz1 + fold(grad), s_dhn + fold(dh1 * normed), s_dh + fold(dh1)

        zero = jnp.zeros((8, width), F32)
        for row, total in zip((0, 2, 3), over_rows(q, norm, (zero, zero, zero))):
            add_vec(row, total)

    def attention_back(h):
        r = rows_of(h)
        dc = dot_t(da_s[r], wo[...]).astype(BF)
        q, k, v = q_s[r], k_s[r], v_s[r]

        def one_head(index, carry):
            dq, dk, dv = carry
            probs = p_s[h * heads + index]
            mine = jnp.where(in_head(index), dc, jnp.zeros_like(dc))
            dp = dot_t(mine, v)
            ds = (probs * (dp - jnp.sum(probs * dp, axis=-1, keepdims=True))).astype(BF)
            dv = jnp.where(in_head(index), tdot(probs.astype(BF), dc), dv)
            dq = jnp.where(in_head(index), dot(ds, k), dq)
            dk = jnp.where(in_head(index), tdot(ds, q), dk)
            return dq, dk, dv

        dq, dk, dv = lax.fori_loop(0, heads, one_head, (jnp.zeros((half, columns), F32),) * 3)
        dq = (dq * scale).astype(BF)
        dk = (dk * scale).astype(BF)
        dv = dv.astype(BF)
        dq_s[r], dk_s[r], dv_s[r] = dq, dk, dv
        add_vec(7, jnp.sum(dq.astype(F32), axis=0, keepdims=True))
        add_vec(8, jnp.sum(dv.astype(F32), axis=0, keepdims=True))

    def grads_a():
        for i, source in enumerate((dq_s, dk_s, dv_s)):
            gap[i * columns : (i + 1) * columns] = tdot(source[...], x[...]).astype(BF)
        gap[3 * columns : 4 * columns] = tdot(ctx_s[...], da_s[...]).astype(BF)

    def back_terms(h):
        r = rows_of(h)
        total = dot(dq_s[r], wq[0 * columns : 1 * columns]) + dot(dk_s[r], wq[1 * columns : 2 * columns]) + dot(dv_s[r], wq[2 * columns : 3 * columns])
        bt[r] = total.astype(BF)

    def moment_copy(index):
        moment = (mq, mo, mu, md)[index]
        return pltpu.make_async_copy(moment, f1.at[pl.ds(0, sizes[index])], lsem.at[0])

    def fetch_moment():
        for index in range(4):
            pl.when(which == PLACE[index])(moment_copy(index).start)

    def cols(index):
        return pl.ds(pl.multiple_of(index * tile, tile), tile)

    def place_of(side, j):
        return side * (1 + j // 2), j + side * (1 - j // 2)

    def gram(indices):
        for index in indices:
            rows = sizes[index]
            first = 0 if square else firsts[index]

            @pl.when(which == PLACE[index])
            def _(index=index, first=first, rows=rows):
                moment_copy(index).wait()
                for i in range(3):
                    spot = pl.ds(i * (rows // 3), rows // 3)
                    z = 0.5 * f1[spot] + gf[pl.ds(first + i * (rows // 3), rows // 3)].astype(F32)
                    if index == 2:
                        z = z.T
                        spot = (pl.ds(0, width), spot)
                    zf[spot] = z
                    zh[spot], zl[spot] = cut(z)
                if rows < width:
                    spot = pl.ds(rows, width - rows)
                    zf[spot] = jnp.zeros((width - rows, width), F32)
                    zh[spot] = jnp.zeros((width - rows, width), BF)
                    zl[spot] = jnp.zeros((width - rows, width), BF)

        over = (((0,), (0,)), ((), ()))

        @pl.loop(0, 3)
        def _(j):
            row, col = place_of(core, j)
            gx[:, cols(j)] = dot3(
                zh[:, cols(row)], zl[:, cols(row)], zh[:, cols(col)], zl[:, cols(col)], over
            )

    diagonal = lax.broadcasted_iota(jnp.int32, (tile, tile), 0) == lax.broadcasted_iota(
        jnp.int32, (tile, tile), 1
    )

    def upper():
        def trace(block):
            return jnp.sum(jnp.where(diagonal, block, 0.0))

        def write(rows, across, value):
            af[rows, across] = value
            ah[rows, across], al[rows, across] = cut(value)

        last = jnp.where(core == 1, go[:, 2 * tile :], gp[:, 2 * tile :])
        total = trace(go[:, 0:tile]) + trace(gp[:, 0:tile]) + trace(last)
        inverse = 1.0 / (jnp.sqrt(jnp.full((1, 1), total, F32)) + 1e-07)
        shrink = inverse * inverse
        for source, side in ((go, core), (gp, 1 - core)):
            for j in range(3):
                row, col = place_of(side, j)
                block = source[:, j * tile : (j + 1) * tile] * shrink
                write(cols(row), cols(col), block)
                if j > 0:
                    write(cols(col), cols(row), block.T)

        if square:
            for index, rows in enumerate(sizes):

                @pl.when(which == PLACE[index])
                def _(half_rows=rows // 2):
                    mine = pl.ds(pl.multiple_of(core * half_rows, half_rows), half_rows)
                    xf[0:half_rows] = zf[mine] * inverse
                    if half_rows < share:
                        xf[half_rows:share] = jnp.zeros((share - half_rows, width), F32)

        else:
            rank = p % group
            xf[...] = zf[pl.ds(pl.multiple_of(rank * share, share), share)] * inverse

    def product(left, right, base, base_scale, factor, targets, times):
        (lh, ll), (rh, rl) = left, right
        for i in range(3):
            rows = pl.ds(i * tile, tile)
            for j in range(i, 3):
                across = pl.ds(j * tile, tile)
                value = base_scale * base[rows, across] + factor * times(
                    lh[rows], ll[rows], rh[:, across], rl[:, across]
                )
                parts = (*cut(value), value)
                for target, part in zip(targets, parts):
                    target[rows, across] = part
                if i != j and len(targets) == 2:
                    for target, part in zip(targets, parts):
                        target[across, rows] = part.T
                elif i != j:
                    mirrored = value.T
                    for target, part in zip(targets, (*cut(mirrored), mirrored)):
                        target[across, rows] = part

    def make_d(times=dot3):
        product((ah, al), (ah, al), af, coef_b, coef_c, (dh, dl), times)

    def move_x(times=dot3):
        xh, xl = cut(xf[...])
        xf[...] = coef_a * xf[...] + times(xh, xl, dh[...], dl[...])

    def own_gradient(index, part):
        if index == 2:
            across = pl.ds(pl.multiple_of(core * (width // 2), width // 2), width // 2)
            piece = sizes[index] // (2)
            return gf[pl.ds(part * piece, piece), across]
        piece = sizes[index] // (4)
        first = pl.multiple_of(core * (sizes[index] // 2) + part * piece, piece)
        return gf[pl.ds(first, piece)]

    def own_step(index, part):
        if index == 2:
            piece = sizes[index] // (2 * CUTS)
            return xf[:, pl.ds(part * piece, piece)].T.astype(BF)
        piece = sizes[index] // (4 * CUTS)
        return xf[pl.ds(part * piece, piece)].astype(BF)

    if square:
        spread = square_gather(p, sizes, gall, own_gradient, 1, scratch[42:44])
        collect = square_gather(p, sizes, xo, own_step, CUTS, scratch[44:46])
        early = (which == PLACE[2]) | (which == PLACE[3])
        late = (which == PLACE[0]) | (which == PLACE[1])

    start, mix, settle, pass_on, end = (
        (lambda q, place=place: sums[q][place]()) for place in range(5)
    )

    def round_trip(first, second):
        end(0), first(0), pass_on(1), second(0), settle(2), mix(3), start(0)
        end(1), first(1), pass_on(2), settle(3), second(1), mix(0), start(1)
        end(2), first(2), pass_on(3), second(2), settle(0), mix(1), start(2)
        end(3), first(3), pass_on(0), second(3), settle(1), mix(2), start(3)

    loads[4].wait()
    narrow(0, f4, wq)
    narrow(1, wo_f, wo)
    attention(0)
    start(0), start(1)
    attention(1)
    mix(0), start(2), mix(1), settle(0), start(3)
    narrow(2, f1, wu)
    mix(2), settle(1), pass_on(0)
    narrow(3, f2, wd)
    loads[5].wait()
    outs = [
        pltpu.make_async_copy(source, target, osem.at[i])
        for i, (source, target) in enumerate(((y, y_hbm), (gt, gt_hbm), (gall, gall_hbm)))
    ]
    round_trip(up, down)
    round_trip(out_back, up_back)
    outs[0].start()
    fetch_moment()
    grads_b()
    plane_b[0]()
    end(0), norm_back(0), pass_on(1), settle(2), mix(3)
    plane_b[1]()
    end(1), norm_back(1), pass_on(2), settle(3)
    attention_back(0)
    end(2), norm_back(2), pass_on(3)
    if square:
        plane_b[2]()
    end(3), norm_back(3)
    attention_back(1)
    grads_a()
    plane_a[0]()
    vector[0]()
    if square:
        plane_b[3]()
        plane_a[1]()

        @pl.when(early)
        def _():
            plane_b[4]()
            gram((2, 3))
            line[0]()

        plane_a[2]()
        back_terms(0)
        back_terms(1)

        @pl.when(late)
        def _():
            plane_a[3]()
            plane_b[4]()
            plane_a[4]()
            gram((0, 1))
            line[0]()
            spread[0]()

    else:
        plane_b[2]()
        plane_a[1]()
        back_terms(0)
        back_terms(1)
        plane_b[3]()
        plane_a[2]()
        plane_b[4]()
        plane_a[3]()
        plane_a[4]()
        gram(range(4))
        line[0]()
    vector[1]()
    moved = 0.5 * mh[...] + vec[7:9, 0:columns]
    squares[0:2] = jnp.broadcast_to(jnp.sum(moved * moved, axis=1, keepdims=True), (2, 128))
    moved = 0.5 * mf[...].reshape(1, width) + vec[6:7]
    squares[2:3] = jnp.broadcast_to(jnp.sum(moved * moved, axis=1, keepdims=True), (1, 128))
    squares[3:8] = jnp.zeros((5, 128), F32)
    along[0]()
    if square:
        pl.when(early)(spread[0])
    for place in range(1, 5):
        line[place]()
        if square and place == 2:
            spread[1]()
    swap = remote(go, gp, psem.at[0], psem.at[1], mate)
    swap.start()
    for q in range(2):
        back[q][0]()
    swap.wait()

    upper()

    def one_pass(lh, ll, rh, rl):
        return dot(lh, rh)

    plan = {
        (0, 1): ((1, 0),),
        (0, 2): ((1, 1), (0, 2)),
        (1, 0): ((2, 0), (0, 3)),
        (1, 1): ((2, 1), (1, 2)),
        (1, 2): ((3, 0), (1, 3)),
        (2, 1): ((3, 1), (2, 2)),
        (2, 2): ((2, 3),),
        (3, 0): ((3, 2),),
        (3, 1): ((3, 3),),
    }

    def between(k, place):
        for turn in range(4):
            actions = plan.get((turn, place), ())
            if actions:

                @pl.when(k == turn)
                def _(turn=turn, actions=actions):
                    for action, q in actions:
                        back[q][action]()
                    if square and (turn, place) == (1, 2):
                        spread[2]()

    def sweep(k, carry):
        make_d()
        xh, xl = cut(xf[...])
        xf[...] = coef_a * xf[...] + dot(xh, dh[...])

        @pl.when(k == 3)
        def _():
            xf[...] += dot(xh, dl[...]) + dot(xl, dh[...])

        between(k, 0)
        product((ah, al), (dh, dl), af, coef_a, 1.0, (sh, sl, sf), dot3)
        between(k, 1)
        product((sh, sl), (dh, dl), sf, coef_a, 1.0, (ah, al, af), dot3)
        between(k, 2)
        return carry

    lax.fori_loop(0, 4, sweep, 0)
    if square:
        collect[1]((2, 3))
    make_d()
    move_x()
    for q in range(4):
        back[q][4]()
    gt[...] = (red_s[...].astype(F32) + dz1[...]).astype(BF)
    outs[1].start()
    along[1]()
    if square:

        @pl.when(early)
        def _():
            plane_a[4]()

        collect[0]()
        collect[1]((0, 1))
        spread[3]()
        outs[2].start()
        collect[2]()
        collect[3]()
    else:
        outs[2].start()
        gather_any(p, core, count // 2, mate, xf, xo, scratch[42], scratch[43])
    last = pltpu.make_async_copy(xo, xo_hbm, osem.at[3])
    last.start()
    for moving in (*outs, last):
        moving.wait()


def gather_any(p, core, pairs, mate, xf, xo, asem_s, asem_r):
    pair = p // 2
    share = xf.shape[0]

    def rows_of(device):
        return xo.at[pl.ds(pl.multiple_of(device * share, share), share)]

    def after(k):
        return 2 * ((pair + k) % pairs) + core

    def before(k):
        return 2 * ((pair + pairs - k) % pairs) + core

    def send(k):
        return remote(rows_of(p), rows_of(p), asem_s.at[0, k], asem_r.at[0, k], {"dp": after(k)})

    def hand(k):
        spot = rows_of(before(k))
        return remote(spot, spot, asem_s.at[1, k], asem_r.at[1, k], mate)

    xo[pl.ds(pl.multiple_of(p * share, share), share)] = xf[...].astype(BF)
    for k in range(1, pairs):
        send(k).start()
    hand(0).start()
    for k in range(1, pairs):
        spot = rows_of(before(k))
        remote(spot, spot, asem_s.at[0, k], asem_r.at[0, k], mate).wait_recv()
        hand(k).start()
    for k in range(pairs):
        spot = rows_of(before(k) + 1 - 2 * core)
        remote(spot, spot, asem_s.at[1, k], asem_r.at[1, k], mate).wait_recv()
    for k in range(1, pairs):
        send(k).wait_send()
    for k in range(pairs):
        hand(k).wait_send()


def step(count, tokens, cotangent, segments, small, weights, moments, collective_id):
    rows, width = tokens.shape
    sizes = tuple(moment.shape[0] for moment in moments)
    columns = sizes[1]
    heads = columns // HD
    half = rows // 2
    tile = width // 3
    square = count == 8

    def low(*shape):
        return pltpu.VMEM(shape, BF)

    def full(*shape):
        return pltpu.VMEM(shape, F32)

    def out(shape, dtype):
        return jax.ShapeDtypeStruct(shape, dtype)

    plane = reduce_scratch if square else functools.partial(plane_scratch, count)
    pair_sems = [pltpu.SemaphoreType.DMA((2, count // 2))] * 2
    steps_rows = sum(sizes) if square else 4 * width
    scratch = (
        [low(rows, width)] * 2
        + [low(steps_rows, width), low(sum(sizes), width)]
        + [low(rows, width)] * 2
        + [full(width, width)] * 3
        + [full(3 * columns, width), full(columns, width)]
        + [full(tile, width)] * 3
        + [full(rows, width)]
        + [low(width, width)] * 8
        + [low(rows, width)] * 2
        + [low(width, width) if square else low(16, width)]
        + [low(4 * columns, width), low(2 * width, width)]
        + [low(3 * columns, width), low(columns, width)]
        + [low(rows, columns)] * 7
        + [full(2 * heads, half, half), full(rows, 128), full(16, width), full(8, 128)]
        + [pltpu.SemaphoreType.DMA((n,)) for n in (6, 2, 2, 4)]
        + relay_scratch(rows // 4, width, BF) * 4
        + plane(2 * width, width)
        + plane(4 * columns, width)
        + vector_scratch(count, (16, width))
        + vector_scratch(4, (8, 128))
        + line_scratch(tile, width, F32)
        + (gather_scratch() * 2 if square else pair_sems)
    )
    return pl.pallas_call(
        functools.partial(step_kernel, count, sizes),
        out_shape=(
            out((rows, width), BF),
            out((rows, width), BF),
            out((steps_rows, width), BF),
            out((sum(sizes), width), BF),
            out((16, width), F32),
            out((8, 128), F32),
        ),
        in_specs=[IN_VMEM] * 6 + [IN_HBM] * 10,
        out_specs=(IN_HBM,) * 4 + (IN_VMEM,) * 2,
        scratch_shapes=scratch,
        compiler_params=params(collective_id, 61),
        name="step",
    )(segments, *small, tokens, cotangent, *weights, *moments)


def apply_kernel(factors, *refs):
    ins, outs = refs[:26], refs[26:]
    small_in, small_out = ins[18:], outs[14:]
    for index, factor in enumerate(factors):
        weight, moment, grad, step = (ins[4 * index + i] for i in range(4))
        new_moment, new, low = (outs[3 * index + i] for i in range(3))
        new_moment[...] = 0.5 * moment[...] + grad[...].astype(F32)
        value = weight[...] - factor * step[...].astype(F32)
        new[...] = value
        low[...] = value.astype(BF)
    for source, target in zip(ins[16:18], outs[12:14]):
        target[...] = source[...]

    @pl.when(pl.program_id(0) == 0)
    def _():
        vec, totals, heads, ff, rows, mom_heads, mom_ff, mom_rows = small_in
        columns = heads.shape[1]
        wide = ff.shape[0]
        moment = 0.5 * mom_heads[...] + vec[7:9, 0:columns]
        small_out[0][...] = moment
        scale = lax.rsqrt(totals[0:2, 0:1] * (1.0 / (4 * columns)) + 1e-06)
        small_out[1][...] = heads[...] - 0.1 * moment * scale
        moment = 0.5 * mom_ff[...].reshape(1, wide) + vec[6:7]
        small_out[2][...] = moment.reshape(wide)
        scale = lax.rsqrt(totals[2:3, 0:1] * (1.0 / (4 * wide)) + 1e-06)
        value = ff[...].reshape(1, wide) - 0.1 * moment * scale
        small_out[3][...] = value.reshape(wide)
        moment = 0.5 * mom_rows[...] + vec[0:6]
        small_out[4][...] = moment
        mean = jnp.mean(moment * moment, axis=-1, keepdims=True)
        small_out[5][...] = rows[...] - 0.1 * moment * lax.rsqrt(mean + 1e-06)


APPLY_STEPS = 4


def apply(sizes, factors, weights, moments, grads, steps, passed, small):
    width = grads.shape[1]
    in_specs, operands, out_specs, out_shape = [], [], [], []

    def block(rows, first=0):
        share = rows // APPLY_STEPS
        return pl.BlockSpec((share, width), lambda i, skip=first // share: (skip + i, 0))

    def whole(array):
        return pl.BlockSpec(array.shape, lambda i, n=array.ndim: (0,) * n)

    first = 0
    for rows, weight, moment in zip(sizes, weights, moments):
        in_specs += [block(rows), block(rows), block(rows, first), block(rows, first)]
        operands += [weight, moment, grads, steps]
        out_specs += [block(rows)] * 3
        out_shape += [jax.ShapeDtypeStruct((rows, width), kind) for kind in (F32, F32, BF)]
        first += rows
    for array in passed:
        turn = pl.BlockSpec((array.shape[0] // 4, width), lambda i: (i // (APPLY_STEPS // 4), 0))
        in_specs.append(turn)
        operands.append(array)
        out_specs.append(turn)
        out_shape.append(jax.ShapeDtypeStruct(array.shape, array.dtype))
    for array in small:
        in_specs.append(whole(array))
        operands.append(array)
    for array in small[2:5]:
        for _ in range(2):
            out_specs.append(whole(array))
            out_shape.append(jax.ShapeDtypeStruct(array.shape, F32))
    return pl.pallas_call(
        functools.partial(apply_kernel, factors),
        grid=(APPLY_STEPS,),
        out_shape=tuple(out_shape),
        in_specs=in_specs,
        out_specs=tuple(out_specs),
        compiler_params=pltpu.CompilerParams(vmem_limit_bytes=61 * 1024 * 1024),
        name="apply",
    )(*operands)


def vector_step(param, moment, mean_sq):
    return param - 0.1 * moment * lax.rsqrt(mean_sq + 1e-06)


def local(
    tokens, segments, cotangent,
    w_qkv, w_out, w_up, w_down, head_bias, ff_bias, row_params,
    mom_qkv, mom_out, mom_up, mom_down, mom_heads, mom_ff, mom_params,
):
    width = tokens.shape[1]
    columns = w_qkv.shape[2]
    ff_cols = w_up.shape[1]
    tensor_size = lax.axis_size("tensor")
    count = lax.axis_size("dp")
    qkv_rows = 3 * columns
    wq_rows = w_qkv.transpose(0, 2, 1).reshape(qkv_rows, width)
    moments = (mom_qkv.transpose(0, 2, 1).reshape(qkv_rows, width), mom_out, mom_up, mom_down)
    output_rows, grad_inputs, steps, grads, vector_total, totals = step(
        count, tokens, cotangent, segments, (row_params, head_bias, ff_bias, mom_heads, mom_ff),
        (wq_rows, w_out, w_up, w_down), moments, 1,
    )

    def to_qkv(rows):
        return rows.reshape(3, columns, width).transpose(0, 2, 1)

    bounds = (0, qkv_rows, qkv_rows + columns, qkv_rows + columns + width)

    def grad_of(index, rows):
        return grads[bounds[index] : bounds[index] + rows].astype(F32)

    def step_of(index, rows):
        first = PLACE[index] * width
        part = steps[first : first + rows].astype(F32)
        return part.T if index == 2 else part

    wide = math.sqrt(ff_cols * tensor_size / width)
    if count == 8:
        sizes = (qkv_rows, columns, width, ff_cols)
        factors = (0.8 * math.sqrt(3.0), 0.8, 0.8 * wide, 0.8 * wide)
        done = apply(
            sizes, factors, (wq_rows, w_out, w_up, w_down), moments, grads, steps, (output_rows, grad_inputs),
            (
                vector_total, totals, head_bias, ff_bias, row_params,
                mom_heads, mom_ff, mom_params,
            ),
        )
        qkv_new = [rows.reshape(3, columns, width).transpose(0, 2, 1) for rows in done[0:3]]
        return (
            *done[12:14], *qkv_new, *done[3:12], *done[14:20],
        )

    new_mom_heads = 0.5 * mom_heads + vector_total[7:9, :columns]
    new_mom_ff = 0.5 * mom_ff + vector_total[6]
    new_mom_params = 0.5 * mom_params + vector_total[0:6]
    new_mom_qkv = 0.5 * mom_qkv + to_qkv(grad_of(0, qkv_rows))
    new_mom_out = 0.5 * mom_out + grad_of(1, columns)
    new_mom_up = 0.5 * mom_up + grad_of(2, width)
    new_mom_down = 0.5 * mom_down + grad_of(3, ff_cols)
    new_qkv = w_qkv - 0.8 * math.sqrt(3.0) * to_qkv(step_of(0, qkv_rows))
    new_out = w_out - 0.8 * step_of(1, columns)
    new_up = w_up - 0.8 * wide * step_of(2, width)
    new_down = w_down - 0.8 * wide * step_of(3, ff_cols)
    new_heads = vector_step(head_bias, new_mom_heads, totals[0:2, 0:1] / (columns * tensor_size))
    new_ff = vector_step(ff_bias, new_mom_ff, totals[2, 0] / (ff_cols * tensor_size))
    new_params = vector_step(
        row_params,
        new_mom_params,
        jnp.mean(new_mom_params * new_mom_params, axis=-1, keepdims=True),
    )
    return (
        output_rows,
        grad_inputs,
        new_mom_qkv, new_qkv, new_qkv.astype(BF),
        new_mom_out, new_out, new_out.astype(BF),
        new_mom_up, new_up, new_up.astype(BF),
        new_mom_down, new_down, new_down.astype(BF),
        new_mom_heads, new_heads,
        new_mom_ff, new_ff,
        new_mom_params, new_params,
    )


def solution(mesh):
    placed = (
        P("dp", None), P("dp", None), P("dp", None),
        P(None, None, "tensor"), P("tensor", None), P(None, "tensor"), P("tensor", None),
        P(None, "tensor"), P("tensor"), P(),
        P(None, None, "tensor"), P("tensor", None), P(None, "tensor"), P("tensor", None),
        P(None, "tensor"), P("tensor"), P(),
    )
    triple = ((P(None, None, "tensor"),) * 3, (P("tensor", None),) * 3, (P(None, "tensor"),) * 3)
    return jax.shard_map(
        local,
        mesh=mesh,
        in_specs=placed,
        out_specs=(
            (P("dp", None), P("dp", None))
            + triple[0] + triple[1] + triple[2] + triple[1]
            + (P(None, "tensor"), P(None, "tensor"), P("tensor"), P("tensor"), P(), P())
        ),
        check_vma=False,
    )
```

profile of v0, /device:TPU:13, one launch (start us, length us, event | category | flops | bytes accessed | tf_op | source)
XLA Modules:
  0.0 209.9 jit_solution(6977640331783152694)
XLA Ops:
  0.7 195.0 %step.1 = (bf16[512,768]{1,0:T(8,128)(2,1)}, bf16[512,768]{1,0:T(8,128)(2,1)}, bf16[2304,768]{1,0:T(8,128)(2,1)}, bf16[2304,768]{1,0:T(8,128)(2,1)}, f32[16,768]{1,0:T(8,128)}, /*index=5*/f32[8,128]{1,0:T(8,128)}) custom-call(s32[2,256]{1,0:T(2,128)} %seg.1, f32[6,768]{1,0:T(8,128)} %refs_22_.1, f32[2,192]{1,0:T(2,128)} %refs_20_.1, f32[768]{0:T(1024)} %refs_21_.1, ...), custom_call_target="tpu_custom_call" | custom-call | tf_op jit(solution)/shard_map/step/pallas_call | solution.py:1330
  195.7 14.0 %apply.1 = (f32[576,768]{1,0:T(8,128)}, f32[576,768]{1,0:T(8,128)}, bf16[576,768]{1,0:T(8,128)(2,1)}, f32[192,768]{1,0:T(8,128)}, f32[192,768]{1,0:T(8,128)}, /*...) custom-call(f32[576,768]{1,0:T(8,128)} %bitcast.16, ...), custom_call_target="tpu_custom_call" | custom-call | tf_op jit(solution)/shard_map/apply/pallas_call | solution.py:1415
where the time goes:
time: 211 us; the launch traced here: 210 us
  Pallas kernels  209 us (99%)
    pallas_call x1, Pallas kernels, step(): pl.pallas_call(functools.partial(step_kernel, count, sizes), out_shape=(o...  195 us
    pallas_call x1, Pallas kernels, apply(): pl.pallas_call(functools.partial(apply_kernel, factors), grid=(APPLY_STEP...  14 us

commit v1 on v0

--- a/solution.py
+++ b/solution.py
@@ -19,6 +19,7 @@
 SUBS = 2
 PLACE = (1, 2, 0, 3)
 CUTS = 3
+LAST_FIRST = (2, 3, 1, 0)
 
 
 def remote(src, dst, send_sem, recv_sem, device):
@@ -613,7 +614,7 @@
                         copy(index, part, 3, mate).start()
 
     def rest():
-        for index in range(4):
+        for index in LAST_FIRST:
             for away, route, _ in ways:
 
                 @role(index, away)
@@ -628,10 +629,14 @@
                     wait_in(index, part, 2, core)
                     copy(index, part, 3, mate).start()
 
-    def finish():
+    def finish(ready=None):
+        for index in LAST_FIRST:
+            for part in range(parts):
+                wait_in(index, part, 3, 1 - core)
+            if index == 1 and ready is not None:
+                ready()
         for index in range(4):
             for part in range(parts):
-                wait_in(index, part, 3, 1 - core)
                 copy(index, part, 3, mate).wait_send()
 
             @role(index, 0)
@@ -1231,16 +1236,22 @@
             plane_a[4]()
 
         collect[0]()
-        collect[1]((0, 1))
+        collect[1]((1, 0))
         spread[3]()
         outs[2].start()
         collect[2]()
-        collect[3]()
+        rest = pl.ds(sizes[0], sum(sizes[1:]))
+        most = pltpu.make_async_copy(xo.at[rest], xo_hbm.at[rest], osem.at[4])
+        collect[3](most.start)
+        first = pl.ds(0, sizes[0])
+        last = pltpu.make_async_copy(xo.at[first], xo_hbm.at[first], osem.at[3])
+        last.start()
+        most.wait()
     else:
         outs[2].start()
         gather_any(p, core, count // 2, mate, xf, xo, scratch[42], scratch[43])
-    last = pltpu.make_async_copy(xo, xo_hbm, osem.at[3])
-    last.start()
+        last = pltpu.make_async_copy(xo, xo_hbm, osem.at[3])
+        last.start()
     for moving in (*outs, last):
         moving.wait()
 
@@ -1318,7 +1329,7 @@
         + [low(3 * columns, width), low(columns, width)]
         + [low(rows, columns)] * 7
         + [full(2 * heads, half, half), full(rows, 128), full(16, width), full(8, 128)]
-        + [pltpu.SemaphoreType.DMA((n,)) for n in (6, 2, 2, 4)]
+        + [pltpu.SemaphoreType.DMA((n,)) for n in (6, 2, 2, 5)]
         + relay_scratch(rows // 4, width, BF) * 4
         + plane(2 * width, width)
         + plane(4 * columns, width)

time: 211 us -> 209 us (level)
  no operation moved by 1% of the time
where the time goes in v1:
time: 209 us; the launch traced here: 208 us
  Pallas kernels  207 us (99%)
    pallas_call x1, Pallas kernels, step(): pl.pallas_call(functools.partial(step_kernel, count, sizes), out_shape=(o...  193 us
    pallas_call x1, Pallas kernels, apply(): pl.pallas_call(functools.partial(apply_kernel, factors), grid=(APPLY_STEP...  14 us

profile of v1, /device:TPU:13, one launch (start us, length us, event | category | flops | bytes accessed | tf_op | source)
XLA Modules:
  0.0 208.3 jit_solution(11915626607228879967)
XLA Ops:
  0.7 193.4 %step.1 = (bf16[512,768]{1,0:T(8,128)(2,1)}, bf16[512,768]{1,0:T(8,128)(2,1)}, bf16[2304,768]{1,0:T(8,128)(2,1)}, bf16[2304,768]{1,0:T(8,128)(2,1)}, f32[16,768]{1,0:T(8,128)}, /*index=5*/f32[8,128]{1,0:T(8,128)}) custom-call(s32[2,256]{1,0:T(2,128)} %seg.1, f32[6,768]{1,0:T(8,128)} %refs_22_.1, f32[2,192]{1,0:T(2,128)} %refs_20_.1, f32[768]{0:T(1024)} %refs_21_.1, ...), custom_call_target="tpu_custom_call" | custom-call | tf_op jit(solution)/shard_map/step/pallas_call | solution.py:1341
  194.1 14.0 %apply.1 = (f32[576,768]{1,0:T(8,128)}, f32[576,768]{1,0:T(8,128)}, bf16[576,768]{1,0:T(8,128)(2,1)}, f32[192,768]{1,0:T(8,128)}, f32[192,768]{1,0:T(8,128)}, /*...) custom-call(f32[576,768]{1,0:T(8,128)} %bitcast.16, ...), custom_call_target="tpu_custom_call" | custom-call | tf_op jit(solution)/shard_map/apply/pallas_call | solution.py:1426
